TPU v7x, 32 devices: a whole 2x2x4 slice. The times are simulated.
32 devices in a mesh: groups: 2 (over y), dp: 16 (over z, x, core).
Axes of the slice: x: 2, y: 2, z: 4, core: 2. Of those that a mesh axis runs over, the one named last changes fastest.
Arguments:
- merger_input: bfloat16 [3072, 2304], P(('groups', 'dp')), parts along dimension 0, may hold values from -6 to 6
- merger_weight: bfloat16 [2304, 2048], P('dp'), may hold values from -0.125 to 0.125
- merger_bias: float32 [2048], replicated, may hold values from -3 to 3
- norm_gain: float32 [2048], replicated, may hold values from 0.5 to 1.5
- gate_weight: bfloat16 [16, 2048, 768], P('dp'), may hold values from -0.125 to 0.125
- up_weight: bfloat16 [16, 2048, 768], P('dp'), may hold values from -0.125 to 0.125
- down_weight: bfloat16 [16, 768, 2048], P('dp'), may hold values from -0.21875 to 0.21875
- expert_ids: int32 [3072, 8], P(('groups', 'dp')), parts along dimension 0, may hold values from 0 to 15, all different within a row; in each aligned block of 96 rows (0 to 95, 96 to 191, ...) at most 72 rows name the same one
- combine_ints: int32 [3072, 8], P(('groups', 'dp')), parts along dimension 0, may hold values from 1 to 16
Outputs:
- mixed: bfloat16 [3072, 2048], P(('groups', 'dp')), parts along dimension 0
There are 2 independent parts, one for each index of `groups`. A program takes and returns all parts, laid end to end along the dimension named above; an argument that names none is the same for every part. Nothing has to cross between parts.
Inputs may be any that keep to these rules, and one draw needn't show every extreme that they name: `expert_ids`: each row names 8 different experts; in the rows of one device no expert is named more than 72 times, and that many is reached.
All inputs are finite; a program needn't handle non-finite values.
Results may differ from a plain program's by a relative error of at most 0.0051.
Values may be sent and summed in bfloat16 or wider, within the bound.
A program may use at most 128 MiB of HBM per device.

v0:
```python
import jax
import jax.numpy as jnp
from jax import lax
from jax.sharding import PartitionSpec as P


def run_experts(received, gate_weight, up_weight, down_weight, ndevices):
    local = gate_weight.shape[0]
    slots = received.shape[1]
    width = received.shape[2]
    inputs = received.reshape(ndevices, local, slots, width)
    gate = jnp.einsum("jlcd,ldh->jlch", inputs, gate_weight, preferred_element_type=jnp.float32)
    up = jnp.einsum("jlcd,ldh->jlch", inputs, up_weight, preferred_element_type=jnp.float32)
    hidden = (jax.nn.silu(gate) * up).astype(jnp.bfloat16)
    output = jnp.einsum("jlch,lhd->jlcd", hidden, down_weight, preferred_element_type=jnp.float32)
    return output.astype(jnp.bfloat16).reshape(ndevices * local, slots, width)


def shards(
    merger_input,
    merger_weight,
    merger_bias,
    norm_gain,
    gate_weight,
    up_weight,
    down_weight,
    expert_ids,
    combine_ints,
):
    ndevices = lax.axis_size("dp")
    rows = merger_input.shape[0]
    width = merger_weight.shape[1]
    choose = expert_ids.shape[1]
    experts_all = gate_weight.shape[0] * ndevices
    capacity = (3 * rows * choose + 2 * ndevices - 1) // (2 * ndevices)
    act = jax.nn.gelu(merger_input.astype(jnp.float32), approximate=False).astype(jnp.bfloat16)
    merged = jnp.dot(
        act,
        lax.all_gather(merger_weight, "dp", axis=0, tiled=True),
        preferred_element_type=jnp.float32,
    )
    merged = merged + merger_bias
    scale = lax.rsqrt(jnp.mean(merged * merged, axis=1, keepdims=True) + 1e-06)
    normed = (merged * scale * norm_gain).astype(jnp.bfloat16)
    onehot = (
        expert_ids[:, :, None] == jnp.arange(experts_all, dtype=jnp.int32)[None, None, :]
    ).astype(jnp.int32)
    flat_hot = onehot.reshape(rows * choose, experts_all)
    before = jnp.cumsum(flat_hot, axis=0) - flat_hot
    position = jnp.sum(before * flat_hot, axis=1)
    slot_flat = expert_ids.reshape(rows * choose) * capacity + position
    repeated = jnp.repeat(normed, choose, axis=0)
    outgoing = jnp.zeros((experts_all * capacity, width), jnp.bfloat16).at[slot_flat].set(repeated)
    outgoing = outgoing.reshape(experts_all, capacity, width)
    received = lax.all_to_all(outgoing, "dp", split_axis=0, concat_axis=0, tiled=True)
    served = run_experts(received, gate_weight, up_weight, down_weight, ndevices)
    returned = lax.all_to_all(served, "dp", split_axis=0, concat_axis=0, tiled=True)
    returned = returned.reshape(experts_all * capacity, width)
    picked = returned[slot_flat].reshape(rows, choose, width)
    counts = combine_ints.astype(jnp.float32)
    weights = counts / jnp.sum(counts, axis=1, keepdims=True)
    combined = jnp.sum(weights[:, :, None] * picked.astype(jnp.float32), axis=1)
    return (merged + combined).astype(jnp.bfloat16)


def solution(mesh):
    placed = (
        P(("groups", "dp"), None),
        P("dp", None),
        P(),
        P(),
        P("dp", None, None),
        P("dp", None, None),
        P("dp", None, None),
        P(("groups", "dp"), None),
        P(("groups", "dp"), None),
    )
    return jax.shard_map(
        shards, mesh=mesh, in_specs=placed, out_specs=P(("groups", "dp"), None), check_vma=False
    )
```

profile of v0, /device:TPU:11, one launch (start us, length us, event | category | flops | bytes accessed | tf_op | source)
XLA Modules:
  0.0 371.1 jit_solution(13952559320451286029)
XLA Ops:
  6.5 0.7 all-gather.2.cloned.1.call-update
  7.3 1.0 copy.13
  8.3 0.1 eq.30
  8.5 1.7 reduce-window.6
  10.2 0.3 slice_reduce_fusion
  10.5 0.7 broadcast_multiply_fusion
  11.1 0.1 copy.12
  11.2 0.1 mul.76
  11.3 0.1 fusion.85
  11.5 79.4 %all-gather.2.cloned.1.call-done = bf16[2304,2048]{1,0:T(8,128)(2,1)} async-done(((bf16[144,2048]{1,0:T(8,128)(2,1)}), bf16[2304,2048]{1,0:T(8,128)(2,1)}) %all-gather.2.cloned.1.call-update) | async-done | bytes 9437200 | tf_op jit(solution)/shard_map/all_gather | solution.py:39
  90.9 7.1 %multiply_reduce_fusion = (f32[96]{0:T(128)S(1)}, f32[96,2048]{1,0:T(8,128)S(1)}) fusion(f32[2048]{0:T(1024)} %param.11, bf16[2304,2048]{1,0:T(8,128)(2,1)} %all-gather.2.cloned.1.call-done, bf16[96,2304]{1,0:T(8,128)(2,1)} %param.9), kind=kOutput, calls=%fused_computation.59 | convolution fusion | flops 921157504 | bytes 10674560 | tf_op jit(solution)/shard_map/dot_general | solution.py:37
  98.0 0.9 copy-done.2
  98.9 0.1 multiply_convert_fusion
  99.1 9.6 %scatter_custom_fusion = bf16[1152,2048]{1,0:T(8,128)(2,1)} fusion(s32[768]{0:T(1024)S(1)} %fusion.87, bf16[]{:T(256)} %constant.31.clone.1, bf16[96,2048]{1,0:T(8,128)(2,1)S(1)} %multiply_convert_fusion), kind=kCustom, calls=%fused_computation.17 | custom fusion | bytes 5111810 | tf_op jit(solution)/shard_map/scatter | solution.py:53
  108.7 109.6 %all_to_all.10 = bf16[16,72,2048]{2,1,0:T(8,128)(2,1)S(1)} all-to-all(bf16[16,72,2048]{2,1,0:T(8,128)(2,1)} %bitcast.85), channel_id=1, replica_groups=mesh['groups'=2,'dp'=16] {'dp'}, dimensions={0} | all-to-all | bytes 9437184 | tf_op jit(solution)/shard_map/all_to_all | solution.py:55
  218.3 2.2 copy-done.1
  220.4 5.7 %fusion.6 = f32[16,72,768]{2,1,0:T(8,128)} fusion(bf16[16,72,2048]{2,1,0:T(8,128)(2,1)S(1)} %all_to_all.10, bf16[1,2048,768]{2,1,0:T(8,128)(2,1)S(1)} %copy-done.6), kind=kOutput, calls=%fused_computation.13 | convolution fusion | flops 3623878656 | bytes 11403264 | tf_op jit(solution)/shard_map/jlcd,ldh->jlch/dot_general | solution.py:13
  226.2 13.5 %convolution_convert_fusion = bf16[16,72,2048]{2,1,0:T(8,128)(2,1)} fusion(bf16[1,768,2048]{2,1,0:T(8,128)(2,1)S(1)} %copy-done, f32[16,72,768]{2,1,0:T(8,128)} %fusion.6, bf16[16,72,2048]{2,1,0:T(8,128)(2,1)} %copy-done.1, bf16[1,2048,768]{2,1,0:T(8,128)(2,1)} %param.13), kind=kOutput, calls=%fused_computation.4 | convolution fusion | flops 7255425024 | bytes 19267584 | tf_op jit(solution)/shard_map/jlch,lhd->jlcd/dot_general | solution.py:15
  239.7 5.0 %all-to-all-start.1 = ((bf16[16,72,2048]{2,1,0:T(8,128)(2,1)}), bf16[16,72,2048]{2,1,0:T(8,128)(2,1)}, u32[]{:S(2)}, u32[]{:S(2)}) async-start(bf16[16,72,2048]{2,1,0:T(8,128)(2,1)} %convolution_convert_fusion), calls=%async_computation.1 | async-start | bytes 9437184 | tf_op jit(solution)/shard_map/all_to_all | solution.py:57
  244.7 0.1 copy.11
  244.8 103.6 %all-to-all-done.1 = bf16[16,72,2048]{2,1,0:T(8,128)(2,1)} async-done(((bf16[16,72,2048]{2,1,0:T(8,128)(2,1)}), bf16[16,72,2048]{2,1,0:T(8,128)(2,1)}, u32[]{:S(2)}, u32[]{:S(2)}) %all-to-all-start.1) | async-done | bytes 4718624 | tf_op jit(solution)/shard_map/all_to_all | solution.py:57
  348.4 10.0 %gather_fusion = bf16[768,2048]{1,0:T(8,128)(2,1)} fusion(bf16[1152,2048]{1,0:T(8,128)(2,1)} %bitcast.18, s32[1024]{0:T(1024)S(1)} %pad_clamp_fusion), kind=kCustom, calls=%fused_computation | custom fusion | bytes 6294528 | tf_op jit(solution)/shard_map/gather | solution.py:59
  358.5 5.0 %fusion = f32[96,2048]{1,0:T(8,128)S(1)} fusion(bf16[768,2048]{1,0:T(8,128)(2,1)} %gather_fusion, f32[96,8]{1,0:T(8,128)S(1)} %copy.11), kind=kLoop, calls=%fused_computation.3 | loop fusion | flops 4521984 | bytes 3935232 | tf_op jit(solution)/shard_map/reduce_sum | solution.py:62
  363.4 0.8 add_convert_fusion
  (21 shorter events, 0.2 us)
Async XLA Ops:
  6.5 219.6 %copy-start = (bf16[1,768,2048]{2,1,0:T(8,128)(2,1)S(1)}, bf16[1,768,2048]{2,1,0:T(8,128)(2,1)}, u32[]{:S(2)}) copy-start(bf16[1,768,2048]{2,1,0:T(8,128)(2,1)} %param.15) | copy-start | bytes 9437188
  6.5 84.4 %all-gather.2.cloned.1.call-start = ((), (), s32[]{:S(2)}) async-start(), calls=%async_computation.2 | async-start | bytes 10027008 | tf_op jit(solution)/shard_map/all_gather | solution.py:39
  11.5 87.5 %copy-start.5 = (f32[2048]{0:T(1024)S(1)}, f32[2048]{0:T(1024)}, u32[]{:S(2)}) copy-start(f32[2048]{0:T(1024)} %param.12) | copy-start | bytes 24580
  98.0 1.0 copy-start.2
  108.7 111.7 %copy-start.6 = (bf16[1,2048,768]{2,1,0:T(8,128)(2,1)S(1)}, bf16[1,2048,768]{2,1,0:T(8,128)(2,1)}, u32[]{:S(2)}) copy-start(bf16[1,2048,768]{2,1,0:T(8,128)(2,1)} %param.14) | copy-start | bytes 9437188
  218.3 2.2 copy-start.1
  239.7 5.0 %copy-start.4 = (s32[96,8]{0,1:T(8,128)S(1)}, s32[96,8]{0,1:T(8,128)}, u32[]{:S(2)}) copy-start(s32[96,8]{0,1:T(8,128)} %param.17) | copy-start | bytes 9220
  239.7 108.7 %all-to-all-start.1 = ((bf16[16,72,2048]{2,1,0:T(8,128)(2,1)}), bf16[16,72,2048]{2,1,0:T(8,128)(2,1)}, u32[]{:S(2)}, u32[]{:S(2)}) async-start(bf16[16,72,2048]{2,1,0:T(8,128)(2,1)} %convolution_convert_fusion), calls=%async_computation.1 | async-start | bytes 9437184 | tf_op jit(solution)/shard_map/all_to_all | solution.py:57
  358.5 5.0 %copy-start.3 = (f32[96,2048]{1,0:T(8,128)S(1)}, f32[96,2048]{1,0:T(8,128)}, u32[]{:S(2)}) copy-start(f32[96,2048]{1,0:T(8,128)} %copy-done.2) | copy-start | bytes 2359300
Sparse Core Ops, SparseCore 0:
  9.6 81.2 all-gather.1
where the time goes:
time: 371 us
  waiting for transfers between devices  184 us (50%)
  blocking collectives  110 us (30%)
  matrix products  26.3 us (7%)
  local copies, waits for them, and re-layouts  24.5 us (7%)
  between operations  13.5 us (4%)
  other arithmetic  8.52 us (2%)
  starting transfers between devices  5.04 us (1%)
    all_to_all x1, blocking collectives, shards(): lax.all_to_all(outgoing, 'dp', split_axis=0, concat_axis=0, tiled=True)  110 us
    all_to_all x1, waiting for transfers between devices, shards(): lax.all_to_all(served, 'dp', split_axis=0, concat_axis=0, tiled=True)  104 us
    all_gather x1, waiting for transfers between devices, shards(): lax.all_gather(merger_weight, 'dp', axis=0, tiled=True)  79.4 us
    dot_general x1, matrix products, run_experts(): jnp.einsum('jlch,lhd->jlcd', hidden, down_weight, preferred_element_type=...  13.5 us
    gather x1, local copies, waits for them, and re-layouts, shards(): picked = returned[slot_flat].reshape(rows, choose, width)  10 us
    scatter x1, local copies, waits for them, and re-layouts, shards(): jnp.zeros((experts_all * capacity, width), jnp.bfloat16).at[slot_flat]  9.65 us
  transfers between devices with their start and end apart: 2, of which 2 were waited for; matrix products, arithmetic and copies ran while one was open for 1% of the time, Pallas kernels for 0%

commit v1 on v0

v1 whole, which is shorter than its diff:
```python
import functools

import jax
import jax.numpy as jnp
from jax import lax
from jax.experimental import pallas as pl
from jax.experimental.pallas import tpu as pltpu
from jax.sharding import PartitionSpec as P

LANES = 128
VMEM_BYTES = 60 << 20
F32, BF16 = jnp.float32, jnp.bfloat16


def run_experts(received, gate_weight, up_weight, down_weight, ndevices):
    local = gate_weight.shape[0]
    slots = received.shape[1]
    width = received.shape[2]
    inputs = received.reshape(ndevices, local, slots, width)
    gate = jnp.einsum("jlcd,ldh->jlch", inputs, gate_weight, preferred_element_type=F32)
    up = jnp.einsum("jlcd,ldh->jlch", inputs, up_weight, preferred_element_type=F32)
    hidden = (jax.nn.silu(gate) * up).astype(BF16)
    output = jnp.einsum("jlch,lhd->jlcd", hidden, down_weight, preferred_element_type=F32)
    return output.astype(BF16).reshape(ndevices * local, slots, width)


def routed_shards(
    act,
    merger_weight,
    merger_bias,
    norm_gain,
    gate_weight,
    up_weight,
    down_weight,
    expert_ids,
    combine_ints,
):
    ndevices = lax.axis_size("dp")
    rows = act.shape[0]
    width = merger_weight.shape[1]
    choose = expert_ids.shape[1]
    experts_all = gate_weight.shape[0] * ndevices
    capacity = (3 * rows * choose + 2 * ndevices - 1) // (2 * ndevices)
    merged = jnp.dot(
        act,
        lax.all_gather(merger_weight, "dp", axis=0, tiled=True),
        preferred_element_type=F32,
    )
    merged = merged + merger_bias
    scale = lax.rsqrt(jnp.mean(merged * merged, axis=1, keepdims=True) + 1e-06)
    normed = (merged * scale * norm_gain).astype(BF16)
    pairs = rows * choose
    flat = expert_ids.reshape(pairs)
    earlier = jnp.arange(pairs)[:, None] > jnp.arange(pairs)[None, :]
    position = jnp.sum((earlier & (flat[:, None] == flat[None, :])).astype(jnp.int32), axis=1)
    slot_flat = flat * capacity + position
    repeated = jnp.repeat(normed, choose, axis=0)
    outgoing = jnp.zeros((experts_all * capacity, width), BF16).at[slot_flat].set(repeated)
    outgoing = outgoing.reshape(experts_all, capacity, width)
    received = lax.all_to_all(outgoing, "dp", split_axis=0, concat_axis=0, tiled=True)
    served = run_experts(received, gate_weight, up_weight, down_weight, ndevices)
    returned = lax.all_to_all(served, "dp", split_axis=0, concat_axis=0, tiled=True)
    returned = returned.reshape(experts_all * capacity, width)
    picked = returned[slot_flat].reshape(rows, choose, width)
    counts = combine_ints.astype(F32)
    weights = counts / jnp.sum(counts, axis=1, keepdims=True)
    combined = jnp.sum(weights[:, :, None] * picked.astype(F32), axis=1)
    return (merged + combined).astype(BF16)


def fused_kernel(
    n,
    act_ref,
    counts_ref,
    bias_ref,
    gain_ref,
    weight_hbm,
    gate_hbm,
    up_hbm,
    down_hbm,
    out_ref,
    wbuf,
    xbuf,
    part,
    sib,
    from_left,
    from_right,
    gate_v,
    up_v,
    down_v,
    merged,
    hid,
    local_sem,
    w_sems,
    w_sib,
    x_sems,
    x_sib,
    r_sems,
    r_sib,
):
    chips = n // 2
    half = chips // 2
    depth, width = weight_hbm.shape
    rows = counts_ref.shape[0]
    hidden = gate_v.shape[1]
    me = lax.axis_index("dp")
    core, chip = me % 2, me // 2
    x, z = chip % 2, chip // 2
    pos = z * (1 - x) + (chips - 1 - z) * x

    def chip_at(p):
        p = lax.rem(p + chips, chips)
        xx = p // half
        return (p * (1 - xx) + (chips - 1 - p) * xx) * 2 + xx

    right = chip_at(pos + 1) * 2 + core
    left = chip_at(pos - 1) * 2 + core
    sibling = chip * 2 + 1 - core
    sent = []

    def remote(src, dst, sems, where, device):
        return pltpu.make_async_remote_copy(
            src_ref=src,
            dst_ref=dst,
            send_sem=sems.at[(0, *where)],
            recv_sem=sems.at[(1, *where)],
            device_id={"dp": device},
            device_id_type=pl.DeviceIdType.MESH,
        )

    def start(copy):
        copy.start()
        sent.append(copy)

    loads = [
        pltpu.make_async_copy(
            weight_hbm, wbuf.at[chip, pl.ds(core * depth, depth), :], local_sem.at[0]
        ),
        pltpu.make_async_copy(gate_hbm.at[0], gate_v, local_sem.at[1]),
        pltpu.make_async_copy(up_hbm.at[0], up_v, local_sem.at[2]),
        pltpu.make_async_copy(down_hbm.at[0], down_v, local_sem.at[3]),
    ]
    loads[0].start()
    barrier = pltpu.get_barrier_semaphore()
    for device in (left, right, sibling):
        pl.semaphore_signal(
            barrier, inc=1, device_id={"dp": device}, device_id_type=pl.DeviceIdType.MESH
        )
    pl.semaphore_wait(barrier, 3)
    loads[0].wait()

    def gather(buf, tall, sems, sib_sems, work, after_start):
        columns = buf.shape[2]
        cut = width // 2
        spans = ((0, cut), (cut, columns - cut))

        def piece(at, c, q):
            lo, size = spans[q]
            return buf.at[at, pl.ds(c * tall, tall), pl.ds(lo, size)]

        def ring(way, h, q):
            sign = 1 if way == 0 else -1
            at = chip_at(pos - sign * (h - 1))
            return remote(
                piece(at, core, q), piece(at, core, q), sems, (way, h - 1, q),
                right if way == 0 else left,
            )

        def across(at, i, q):
            return remote(piece(at, core, q), piece(at, core, q), sib_sems, (i, q), sibling)

        def goes(way, h, q):
            return h < half or (h == half and q == way)

        def number(way, h):
            return 0 if h == 0 else 2 * half - 1 if h == half else h + way * (half - 1)

        def arrived(at, i):
            for q in range(2):
                lo, size = spans[q]
                ref = buf.at[at, pl.ds((1 - core) * tall, tall), pl.ds(lo, size)]
                remote(ref, ref, sib_sems, (i, q), sibling).wait_recv()

        for q in range(2):
            for way in range(2):
                start(ring(way, 1, q))
        for q in range(2):
            start(across(chip, 0, q))
        after_start()
        for h in range(1, half + 1):
            for q in range(2):
                for way in range(2):
                    if not goes(way, h, q):
                        continue
                    sign = 1 if way == 0 else -1
                    at = chip_at(pos - sign * h)
                    ref = piece(at, core, q)
                    remote(ref, ref, sems, (way, h - 1, q), left).wait_recv()
                    if goes(way, h + 1, q):
                        start(ring(way, h + 1, q))
                    start(across(at, number(way, h), q))
                if h == 1:
                    if q == 0:
                        arrived(chip, 0)
                        work(chip, 0)
                else:
                    at = chip_at(pos - (h - 1) if q == 0 else pos + (h - 1))
                    arrived(at, number(q, h - 1))
                    work(at, number(q, h - 1))
        arrived(chip_at(pos + half), 2 * half - 1)

    tile = 512

    merged[...] = jnp.broadcast_to(bias_ref[...], merged.shape)

    def merge(at, i):
        @pl.loop(0, width // tile)
        def _(j):
            cols = pl.ds(pl.multiple_of(j * tile, tile), tile)
            merged[:, cols] += jnp.dot(act_ref[at], wbuf[at, :, cols], preferred_element_type=F32)

    def load_experts():
        for copy in loads[1:]:
            copy.start()

    gather(wbuf, depth, w_sems, w_sib, merge, load_experts)
    far = chip_at(pos + half)
    merge(far, 0)

    value = merged[...]
    scale = lax.rsqrt(jnp.mean(value * value, axis=1, keepdims=True) + 1e-06)
    mine = pl.ds(core * rows, rows)
    xbuf[chip, mine, pl.ds(0, width)] = (value * scale * gain_ref[...]).astype(BF16)
    xbuf[chip, mine, pl.ds(width, LANES)] = counts_ref[...]

    theirs = pl.ds((1 - core) * rows, rows)

    def swap(at, i):
        return remote(part.at[at, theirs, :], sib.at[at], r_sib, (i,), sibling)

    hid_tile = 256

    def expert(at, i):
        @pl.loop(0, hidden // hid_tile)
        def _(j):
            cols = pl.ds(pl.multiple_of(j * hid_tile, hid_tile), hid_tile)
            block = xbuf[at, :, pl.ds(0, width)]
            gate = jnp.dot(block, gate_v[:, cols], preferred_element_type=F32)
            up = jnp.dot(block, up_v[:, cols], preferred_element_type=F32)
            hid[:, cols] = (jax.nn.silu(gate) * up).astype(BF16)

        counts = xbuf[at, :, pl.ds(width, LANES)].astype(F32)
        lane = lax.broadcasted_iota(jnp.int32, counts.shape, 1)
        factor = jnp.sum(jnp.where(lane == me, counts, 0.0), axis=1, keepdims=True)

        @pl.loop(0, width // tile)
        def _(j):
            cols = pl.ds(pl.multiple_of(j * tile, tile), tile)
            result = jnp.dot(hid[...], down_v[:, cols], preferred_element_type=F32).astype(BF16)
            part[at, :, cols] = (result.astype(F32) * factor).astype(BF16)

        start(swap(at, i))

    def wait_experts():
        for copy in loads[1:]:
            copy.wait()

    gather(xbuf, rows, x_sems, x_sib, expert, wait_experts)

    cut = width // 2

    def span(q):
        return pl.ds(q * cut, cut)

    def landing(way, k):
        return (from_left if way == 0 else from_right).at[k - 1]

    def returned(way, k, q):
        dist = half + 1 - k
        at = chip_at(pos + dist if way == 0 else pos - dist)
        return remote(
            part.at[at, mine, span(q)],
            landing(way, k).at[:, span(q)],
            r_sems,
            (way, k - 1, q),
            right if way == 0 else left,
        )

    def swapped(at, i):
        ref = sib.at[at]
        remote(ref, ref, r_sib, (i,), sibling).wait_recv()

    def landed(way, k, q):
        ref = landing(way, k).at[:, span(q)]
        remote(ref, ref, r_sems, (way, k - 1, q), left).wait_recv()

    def both(at, q):
        return part[at, mine, span(q)].astype(F32) + sib[at, :, span(q)].astype(F32)

    def send(way, k, q, more):
        dist = half + 1 - k
        at = chip_at(pos + dist if way == 0 else pos - dist)
        total = both(at, q)
        if more:
            landed(way, k - 1, q)
            total = total + landing(way, k - 1)[:, span(q)].astype(F32)
        part[at, mine, span(q)] = total.astype(BF16)
        start(returned(way, k, q))

    for way in range(2):
        d = half - 1
        at = chip_at(pos + d if way == 0 else pos - d)
        swapped(at, d + (1 - way) * (half - 1))
        send(way, 2, 1 - way, False)
    expert(far, 2 * half - 1)
    swapped(far, 2 * half - 1)
    for way in range(2):
        send(way, 1, way, False)
    for k in range(2, half + 1):
        dist = half + 1 - k
        if k > 2:
            for way in range(2):
                at = chip_at(pos + dist if way == 0 else pos - dist)
                swapped(at, dist + (1 - way) * (half - 1))
            for way in range(2):
                send(way, k, 1 - way, True)
        for way in range(2):
            send(way, k, way, True)
    swapped(chip, 0)
    inverse = 1.0 / jnp.sum(counts_ref[...].astype(F32), axis=1, keepdims=True)
    for q in range(2):
        total = both(chip, q)
        for way in range(2):
            landed(way, half, q)
            total = total + landing(way, half)[:, span(q)].astype(F32)
        out_ref[:, span(q)] = (merged[:, span(q)] + total * inverse).astype(BF16)
    for copy in sent:
        copy.wait_send()


def fused_shards(
    act, merger_weight, merger_bias, norm_gain, gate_weight, up_weight, down_weight, counts
):
    n = lax.axis_size("dp")
    chips, half = n // 2, n // 4
    rows = act.shape[0]
    depth, width = merger_weight.shape
    hidden = gate_weight.shape[2]
    by_chip = act.reshape(rows, chips, 2 * depth).transpose(1, 0, 2)
    vmem = pl.BlockSpec(memory_space=pltpu.VMEM)
    hbm = pl.BlockSpec(memory_space=pl.ANY)
    dma = pltpu.SemaphoreType.DMA
    return pl.pallas_call(
        functools.partial(fused_kernel, n),
        out_shape=jax.ShapeDtypeStruct((rows, width), BF16),
        in_specs=[vmem] * 4 + [hbm] * 4,
        out_specs=vmem,
        scratch_shapes=[
            pltpu.VMEM((chips, 2 * depth, width), BF16),
            pltpu.VMEM((chips, 2 * rows, width + LANES), BF16),
            pltpu.VMEM((chips, 2 * rows, width), BF16),
            pltpu.VMEM((chips, rows, width), BF16),
            pltpu.VMEM((half, rows, width), BF16),
            pltpu.VMEM((half, rows, width), BF16),
            pltpu.VMEM((width, hidden), BF16),
            pltpu.VMEM((width, hidden), BF16),
            pltpu.VMEM((hidden, width), BF16),
            pltpu.VMEM((rows, width), F32),
            pltpu.VMEM((2 * rows, hidden), BF16),
            dma((4,)),
            dma((2, 2, half, 2)),
            dma((2, chips, 2)),
            dma((2, 2, half, 2)),
            dma((2, chips, 2)),
            dma((2, 2, half, 2)),
            dma((2, chips)),
        ],
        compiler_params=pltpu.CompilerParams(
            collective_id=0, has_side_effects=True, vmem_limit_bytes=VMEM_BYTES
        ),
    )(
        by_chip,
        counts,
        merger_bias[None, :],
        norm_gain[None, :],
        merger_weight,
        gate_weight,
        up_weight,
        down_weight,
    )


def fits(n, rows, depth, width, hidden, local):
    if n % 4 or n < 8 or n > LANES or local != 1 or rows % 16 or depth % 16:
        return False
    if width % 512 or hidden % 256:
        return False
    gathered = n * (depth * width + rows * (width + LANES))
    sums = n * rows * width * 2 + n * rows * width // 2
    rest = 3 * width * hidden + 2 * rows * (hidden + width) + n * rows * depth
    return 2 * (gathered + sums + rest) < VMEM_BYTES - (8 << 20)


def shards(
    merger_input,
    merger_weight,
    merger_bias,
    norm_gain,
    gate_weight,
    up_weight,
    down_weight,
    expert_ids,
    combine_ints,
):
    n = lax.axis_size("dp")
    rows = merger_input.shape[0]
    depth, width = merger_weight.shape
    local, _, hidden = gate_weight.shape
    act = jax.nn.gelu(merger_input.astype(F32), approximate=False).astype(BF16)
    weights = (merger_weight, merger_bias, norm_gain, gate_weight, up_weight, down_weight)
    if not fits(n, rows, depth, width, hidden, local):
        return routed_shards(act, *weights, expert_ids, combine_ints)
    named = expert_ids[:, :, None] == jnp.arange(LANES, dtype=jnp.int32)
    counts = jnp.sum(jnp.where(named, combine_ints[:, :, None], 0), axis=1).astype(BF16)
    return fused_shards(act, *weights, counts)


def solution(mesh):
    placed = (
        P(("groups", "dp"), None),
        P("dp", None),
        P(),
        P(),
        P("dp", None, None),
        P("dp", None, None),
        P("dp", None, None),
        P(("groups", "dp"), None),
        P(("groups", "dp"), None),
    )
    return jax.shard_map(
        shards, mesh=mesh, in_specs=placed, out_specs=P(("groups", "dp"), None), check_vma=False
    )
```

time: 371 us -> 141 us (0.38)
  the two profiles are of different devices: /device:TPU:11 before, /device:TPU:0 now
where the time goes in v1:
time: 141 us
  Pallas kernels  132 us (94%)
  local copies, waits for them, and re-layouts  4.42 us (3%)
  other arithmetic  3.82 us (3%)
    pallas_call x1, Pallas kernels, fused_shards(): pl.pallas_call(functools.partial(fused_kernel, n), out_shape=jax.ShapeDty...  132 us
    convert_element_type x1, other arithmetic, shards(): act = jax.nn.gelu(merger_input.astype(F32), approximate=False).astype(BF16)  2.93 us

profile of v1, /device:TPU:0, one launch (start us, length us, event | category | flops | bytes accessed | tf_op | source)
XLA Modules:
  0.0 140.6 jit_solution(714173104435297011)
XLA Ops:
  0.0 0.0 copy-start
  0.0 2.9 %fusion.1 = bf16[96,2304]{1,0:T(8,128)(2,1)S(1)} fusion(bf16[96,2304]{1,0:T(8,128)(2,1)} %param.9), kind=kLoop, calls=%fused_computation.4 | loop fusion | flops 14598144 | bytes 884736 | tf_op jit(solution)/shard_map/convert_element_type | solution.py:419
  2.9 0.9 reshape.5
  3.8 0.9 copy.19
  4.7 0.8 copy.16
  5.5 0.0 copy-done
  5.5 0.1 copy.17
  5.6 0.3 select_reduce_fusion
  5.9 0.6 convert_element_type.11.counts_ref
  6.5 132.4 %shard_map.91 = bf16[96,2048]{1,0:T(8,128)(2,1)} custom-call(bf16[8,96,288]{2,1,0:T(8,128)(2,1)} %bitcast.5, bf16[96,128]{1,0:T(8,128)(2,1)} %convert_element_type.11.counts_ref, f32[1,2048]{1,0:T(1,128)} %bitcast.6, f32[1,2048]{1,0:T(1,128)} %bitcast.7, bf16[144,2048]{1,0:T(8,128)(2,1)} %weight_hbm.1, bf16[1,2048,768]{2,1,0:T(8,128)(2,1)} %gate_hbm.1, ...), custom_call_target="tpu_custom_call" | custom-call | tf_op jit(solution)/shard_map/pallas_call | solution.py:353
  138.9 1.8 %copy.21 = bf16[96,2048]{1,0:T(8,128)(2,1)} copy(bf16[96,2048]{1,0:T(8,128)(2,1)} %shard_map.91) | data formatting | bytes 786432
Async XLA Ops:
  0.0 5.5 %copy-start = (s32[96,8]{0,1:T(8,128)S(1)}, s32[96,8]{0,1:T(8,128)}, u32[]{:S(2)}) copy-start(s32[96,8]{0,1:T(8,128)} %param.17) | copy-start | bytes 9220

commit v2 on v1

--- a/solution.py
+++ b/solution.py
@@ -9,6 +9,8 @@
 
 LANES = 128
 VMEM_BYTES = 60 << 20
+W_PLAN = ((5, 1, 1), (6, 0, 0))
+X_PLAN = ((8, 0, 0), (8, 1, 0))
 F32, BF16 = jnp.float32, jnp.bfloat16
 
 
@@ -68,10 +70,26 @@
     return (merged + combined).astype(BF16)
 
 
+def cut_up(plan, width, group):
+    unit = width // 16
+    split = unit * sum(size for size, _, shared in plan if shared)
+    bases = (0, width - 2 * split + group * split, width - 2 * split + (1 - group) * split)
+    at, spans, twins = [0, 0], [], []
+    for size, way, shared in plan:
+        lo = at[shared] * unit
+        spans.append((bases[shared] + lo, size * unit, way, shared))
+        if shared:
+            twins.append((bases[2] + lo, size * unit, way, shared))
+        at[shared] += size
+    return spans, twins
+
+
 def fused_kernel(
     n,
-    act_ref,
-    counts_ref,
+    paired,
+    input_ref,
+    ids_ref,
+    ints_ref,
     bias_ref,
     gain_ref,
     weight_hbm,
@@ -79,6 +97,8 @@
     up_hbm,
     down_hbm,
     out_ref,
+    act,
+    cbuf,
     wbuf,
     xbuf,
     part,
@@ -93,6 +113,7 @@
     local_sem,
     w_sems,
     w_sib,
+    w_twin,
     x_sems,
     x_sib,
     r_sems,
@@ -101,8 +122,8 @@
     chips = n // 2
     half = chips // 2
     depth, width = weight_hbm.shape
-    rows = counts_ref.shape[0]
     hidden = gate_v.shape[1]
+    group = lax.axis_index("groups")
     me = lax.axis_index("dp")
     core, chip = me % 2, me // 2
     x, z = chip % 2, chip // 2
@@ -118,13 +139,13 @@
     sibling = chip * 2 + 1 - core
     sent = []
 
-    def remote(src, dst, sems, where, device):
+    def remote(src, dst, sems, where, device_id):
         return pltpu.make_async_remote_copy(
             src_ref=src,
             dst_ref=dst,
             send_sem=sems.at[(0, *where)],
             recv_sem=sems.at[(1, *where)],
-            device_id={"dp": device},
+            device_id=device_id,
             device_id_type=pl.DeviceIdType.MESH,
         )
 
@@ -141,73 +162,103 @@
         pltpu.make_async_copy(down_hbm.at[0], down_v, local_sem.at[3]),
     ]
     loads[0].start()
+    rows = ids_ref.shape[1]
+    named = lax.broadcasted_iota(jnp.int32, (n, rows), 0)
+    total = jnp.zeros((n, rows), jnp.int32)
+    for k in range(ids_ref.shape[0]):
+        total += jnp.where(named == ids_ref[k : k + 1, :], ints_ref[k : k + 1, :], 0)
+    counts = jnp.concatenate([total.astype(F32), jnp.zeros((n, LANES - rows), F32)], axis=1)
+    cbuf[chip, pl.ds(core * n, n), :] = counts.astype(BF16)
     barrier = pltpu.get_barrier_semaphore()
-    for device in (left, right, sibling):
+    others = [{"dp": left}, {"dp": right}, {"dp": sibling}] + ([{"groups": 1 - group}] if paired else [])
+    for device_id in others:
         pl.semaphore_signal(
-            barrier, inc=1, device_id={"dp": device}, device_id_type=pl.DeviceIdType.MESH
+            barrier, inc=1, device_id=device_id, device_id_type=pl.DeviceIdType.MESH
         )
-    pl.semaphore_wait(barrier, 3)
+    pl.semaphore_wait(barrier, len(others))
     loads[0].wait()
 
-    def gather(buf, tall, sems, sib_sems, work, after_start):
-        columns = buf.shape[2]
-        cut = width // 2
-        spans = ((0, cut), (cut, columns - cut))
-
-        def piece(at, c, q):
-            lo, size = spans[q]
+    def gather(buf, tall, spans, twins, sems, sib_sems, twin_sems, work, after_start):
+        count = len(spans)
+        shared = [q for q in range(count) if spans[q][3]]
+
+        def piece(at, c, lo, size):
+            if lo is None:
+                return cbuf.at[at, pl.ds(c * n, n), :]
             return buf.at[at, pl.ds(c * tall, tall), pl.ds(lo, size)]
 
         def ring(way, h, q):
             sign = 1 if way == 0 else -1
-            at = chip_at(pos - sign * (h - 1))
-            return remote(
-                piece(at, core, q), piece(at, core, q), sems, (way, h - 1, q),
-                right if way == 0 else left,
-            )
+            ref = piece(chip_at(pos - sign * (h - 1)), core, *spans[q][:2])
+            return remote(ref, ref, sems, (way, h - 1, q), {"dp": right if way == 0 else left})
 
         def across(at, i, q):
-            return remote(piece(at, core, q), piece(at, core, q), sib_sems, (i, q), sibling)
+            ref = piece(at, core, *(spans + twins)[q][:2])
+            return remote(ref, ref, sib_sems, (i, q), {"dp": sibling})
+
+        def over(at, i, s):
+            ref = piece(at, core, *spans[shared[s]][:2])
+            return remote(ref, ref, twin_sems, (i, s), {"groups": 1 - group})
 
         def goes(way, h, q):
-            return h < half or (h == half and q == way)
+            return h < half or (h == half and spans[q][2] == way)
 
         def number(way, h):
             return 0 if h == 0 else 2 * half - 1 if h == half else h + way * (half - 1)
 
-        def arrived(at, i):
-            for q in range(2):
-                lo, size = spans[q]
-                ref = buf.at[at, pl.ds((1 - core) * tall, tall), pl.ds(lo, size)]
-                remote(ref, ref, sib_sems, (i, q), sibling).wait_recv()
-
-        for q in range(2):
+        def blocks(h):
+            if h == 0:
+                return [(chip, 0)]
+            if h == half:
+                return [(chip_at(pos + half), 2 * half - 1)]
+            return [(chip_at(pos - h), number(0, h)), (chip_at(pos + h), number(1, h))]
+
+        def from_twin(h):
+            for s in range(len(shared)):
+                for at, i in blocks(h):
+                    ref = piece(at, core, *twins[s][:2])
+                    remote(ref, ref, twin_sems, (i, s), {"groups": 1 - group}).wait_recv()
+                    start(across(at, i, count + s))
+
+        def ready(at, i):
+            for q in range(count + len(shared)):
+                ref = piece(at, 1 - core, *(spans + twins)[q][:2])
+                remote(ref, ref, sib_sems, (i, q), {"dp": sibling}).wait_recv()
+            return at, i
+
+        for q in range(count):
             for way in range(2):
                 start(ring(way, 1, q))
-        for q in range(2):
+        for q in range(count + len(shared)):
             start(across(chip, 0, q))
         after_start()
+        behind = 2 if shared else 1
         for h in range(1, half + 1):
-            for q in range(2):
+            todo = blocks(h - behind) if h >= behind else []
+            for q in range(count):
                 for way in range(2):
                     if not goes(way, h, q):
                         continue
-                    sign = 1 if way == 0 else -1
-                    at = chip_at(pos - sign * h)
-                    ref = piece(at, core, q)
-                    remote(ref, ref, sems, (way, h - 1, q), left).wait_recv()
+                    at = chip_at(pos - h if way == 0 else pos + h)
+                    ref = piece(at, core, *spans[q][:2])
+                    remote(ref, ref, sems, (way, h - 1, q), {"dp": left}).wait_recv()
                     if goes(way, h + 1, q):
                         start(ring(way, h + 1, q))
+                    if spans[q][3]:
+                        start(over(at, number(way, h), shared.index(q)))
                     start(across(at, number(way, h), q))
-                if h == 1:
-                    if q == 0:
-                        arrived(chip, 0)
-                        work(chip, 0)
-                else:
-                    at = chip_at(pos - (h - 1) if q == 0 else pos + (h - 1))
-                    arrived(at, number(q, h - 1))
-                    work(at, number(q, h - 1))
-        arrived(chip_at(pos + half), 2 * half - 1)
+                if q == (count - 1) // 2:
+                    if h > 1:
+                        from_twin(h - 1)
+                    if todo:
+                        work(*ready(*todo[0]))
+                if q == count - 1 and len(todo) > 1:
+                    work(*ready(*todo[1]))
+        if shared:
+            for at, i in blocks(half - 1):
+                work(*ready(at, i))
+            from_twin(half)
+        ready(*blocks(half)[0])
 
     tile = 512
 
@@ -217,41 +268,49 @@
         @pl.loop(0, width // tile)
         def _(j):
             cols = pl.ds(pl.multiple_of(j * tile, tile), tile)
-            merged[:, cols] += jnp.dot(act_ref[at], wbuf[at, :, cols], preferred_element_type=F32)
-
-    def load_experts():
+            merged[:, cols] += jnp.dot(act[at], wbuf[at, :, cols], preferred_element_type=F32)
+
+    def prepare():
         for copy in loads[1:]:
             copy.start()
-
-    gather(wbuf, depth, w_sems, w_sib, merge, load_experts)
+        for t in range(chips):
+            value = input_ref[:, t * 2 * depth : (t + 1) * 2 * depth].astype(F32)
+            act[t] = (0.5 * value * (1.0 + lax.erf(value * 0.5**0.5))).astype(BF16)
+
+    spans, twins = cut_up(W_PLAN if paired else X_PLAN, width, group)
+    spans.append((None, None, 0, 0))
+    gather(wbuf, depth, spans, twins, w_sems, w_sib, w_twin, merge, prepare)
     far = chip_at(pos + half)
     merge(far, 0)
 
     value = merged[...]
     scale = lax.rsqrt(jnp.mean(value * value, axis=1, keepdims=True) + 1e-06)
     mine = pl.ds(core * rows, rows)
-    xbuf[chip, mine, pl.ds(0, width)] = (value * scale * gain_ref[...]).astype(BF16)
-    xbuf[chip, mine, pl.ds(width, LANES)] = counts_ref[...]
+    xbuf[chip, mine, :] = (value * scale * gain_ref[...]).astype(BF16)
 
     theirs = pl.ds((1 - core) * rows, rows)
 
     def swap(at, i):
-        return remote(part.at[at, theirs, :], sib.at[at], r_sib, (i,), sibling)
+        return remote(part.at[at, theirs, :], sib.at[at], r_sib, (i,), {"dp": sibling})
 
     hid_tile = 256
+
+    def by_row(at, c, picked):
+        table = cbuf[at, pl.ds(c * n, n), :]
+        sums = lax.dot_general(table, picked, (((0,), (0,)), ((), ())), preferred_element_type=F32)
+        return sums[:rows, :1]
 
     def expert(at, i):
         @pl.loop(0, hidden // hid_tile)
         def _(j):
             cols = pl.ds(pl.multiple_of(j * hid_tile, hid_tile), hid_tile)
-            block = xbuf[at, :, pl.ds(0, width)]
+            block = xbuf[at]
             gate = jnp.dot(block, gate_v[:, cols], preferred_element_type=F32)
             up = jnp.dot(block, up_v[:, cols], preferred_element_type=F32)
             hid[:, cols] = (jax.nn.silu(gate) * up).astype(BF16)
 
-        counts = xbuf[at, :, pl.ds(width, LANES)].astype(F32)
-        lane = lax.broadcasted_iota(jnp.int32, counts.shape, 1)
-        factor = jnp.sum(jnp.where(lane == me, counts, 0.0), axis=1, keepdims=True)
+        picked = (lax.broadcasted_iota(jnp.int32, (n, LANES), 0) == me).astype(F32).astype(BF16)
+        factor = jnp.concatenate([by_row(at, 0, picked), by_row(at, 1, picked)], axis=0)
 
         @pl.loop(0, width // tile)
         def _(j):
@@ -265,7 +324,8 @@
         for copy in loads[1:]:
             copy.wait()
 
-    gather(xbuf, rows, x_sems, x_sib, expert, wait_experts)
+    spans, _ = cut_up(X_PLAN, width, group)
+    gather(xbuf, rows, spans, [], x_sems, x_sib, None, expert, wait_experts)
 
     cut = width // 2
 
@@ -283,16 +343,16 @@
             landing(way, k).at[:, span(q)],
             r_sems,
             (way, k - 1, q),
-            right if way == 0 else left,
+            {"dp": right if way == 0 else left},
         )
 
     def swapped(at, i):
         ref = sib.at[at]
-        remote(ref, ref, r_sib, (i,), sibling).wait_recv()
+        remote(ref, ref, r_sib, (i,), {"dp": sibling}).wait_recv()
 
     def landed(way, k, q):
         ref = landing(way, k).at[:, span(q)]
-        remote(ref, ref, r_sems, (way, k - 1, q), left).wait_recv()
+        remote(ref, ref, r_sems, (way, k - 1, q), {"dp": left}).wait_recv()
 
     def both(at, q):
         return part[at, mine, span(q)].astype(F32) + sib[at, :, span(q)].astype(F32)
@@ -327,7 +387,7 @@
         for way in range(2):
             send(way, k, way, True)
     swapped(chip, 0)
-    inverse = 1.0 / jnp.sum(counts_ref[...].astype(F32), axis=1, keepdims=True)
+    inverse = 1.0 / by_row(chip, core, jnp.ones((n, LANES), BF16))
     for q in range(2):
         total = both(chip, q)
         for way in range(2):
@@ -339,25 +399,35 @@
 
 
 def fused_shards(
-    act, merger_weight, merger_bias, norm_gain, gate_weight, up_weight, down_weight, counts
+    merger_input,
+    merger_weight,
+    merger_bias,
+    norm_gain,
+    gate_weight,
+    up_weight,
+    down_weight,
+    expert_ids,
+    combine_ints,
 ):
     n = lax.axis_size("dp")
     chips, half = n // 2, n // 4
-    rows = act.shape[0]
+    rows = merger_input.shape[0]
+    paired = lax.axis_size("groups") == 2
     depth, width = merger_weight.shape
     hidden = gate_weight.shape[2]
-    by_chip = act.reshape(rows, chips, 2 * depth).transpose(1, 0, 2)
     vmem = pl.BlockSpec(memory_space=pltpu.VMEM)
     hbm = pl.BlockSpec(memory_space=pl.ANY)
     dma = pltpu.SemaphoreType.DMA
     return pl.pallas_call(
-        functools.partial(fused_kernel, n),
+        functools.partial(fused_kernel, n, paired),
         out_shape=jax.ShapeDtypeStruct((rows, width), BF16),
-        in_specs=[vmem] * 4 + [hbm] * 4,
+        in_specs=[vmem] * 5 + [hbm] * 4,
         out_specs=vmem,
         scratch_shapes=[
+            pltpu.VMEM((chips, rows, 2 * depth), BF16),
+            pltpu.VMEM((chips, 2 * n, LANES), BF16),
             pltpu.VMEM((chips, 2 * depth, width), BF16),
-            pltpu.VMEM((chips, 2 * rows, width + LANES), BF16),
+            pltpu.VMEM((chips, 2 * rows, width), BF16),
             pltpu.VMEM((chips, 2 * rows, width), BF16),
             pltpu.VMEM((chips, rows, width), BF16),
             pltpu.VMEM((half, rows, width), BF16),
@@ -368,10 +438,11 @@
             pltpu.VMEM((rows, width), F32),
             pltpu.VMEM((2 * rows, hidden), BF16),
             dma((4,)),
-            dma((2, 2, half, 2)),
-            dma((2, chips, 2)),
-            dma((2, 2, half, 2)),
-            dma((2, chips, 2)),
+            dma((2, 2, half, max(len(W_PLAN), len(X_PLAN)) + 1)),
+            dma((2, chips, 2 * len(W_PLAN) + len(X_PLAN) + 1)),
+            dma((2, chips, len(W_PLAN))),
+            dma((2, 2, half, len(X_PLAN))),
+            dma((2, chips, len(X_PLAN))),
             dma((2, 2, half, 2)),
             dma((2, chips)),
         ],
@@ -379,8 +450,9 @@
             collective_id=0, has_side_effects=True, vmem_limit_bytes=VMEM_BYTES
         ),
     )(
-        by_chip,
-        counts,
+        merger_input,
+        expert_ids.T,
+        combine_ints.T,
         merger_bias[None, :],
         norm_gain[None, :],
         merger_weight,
@@ -391,11 +463,11 @@
 
 
 def fits(n, rows, depth, width, hidden, local):
-    if n % 4 or n < 8 or n > LANES or local != 1 or rows % 16 or depth % 16:
+    if n % 4 or n < 8 or n > LANES or n % 16 or local != 1 or rows % 16 or rows >= LANES or depth % 16:
         return False
-    if width % 512 or hidden % 256:
+    if width % 2048 or hidden % 256:
         return False
-    gathered = n * (depth * width + rows * (width + LANES))
+    gathered = n * (depth * width + rows * width + n * LANES)
     sums = n * rows * width * 2 + n * rows * width // 2
     rest = 3 * width * hidden + 2 * rows * (hidden + width) + n * rows * depth
     return 2 * (gathered + sums + rest) < VMEM_BYTES - (8 << 20)
@@ -416,13 +488,11 @@
     rows = merger_input.shape[0]
     depth, width = merger_weight.shape
     local, _, hidden = gate_weight.shape
+    weights = (merger_weight, merger_bias, norm_gain, gate_weight, up_weight, down_weight)
+    if fits(n, rows, depth, width, hidden, local):
+        return fused_shards(merger_input, *weights, expert_ids, combine_ints)
     act = jax.nn.gelu(merger_input.astype(F32), approximate=False).astype(BF16)
-    weights = (merger_weight, merger_bias, norm_gain, gate_weight, up_weight, down_weight)
-    if not fits(n, rows, depth, width, hidden, local):
-        return routed_shards(act, *weights, expert_ids, combine_ints)
-    named = expert_ids[:, :, None] == jnp.arange(LANES, dtype=jnp.int32)
-    counts = jnp.sum(jnp.where(named, combine_ints[:, :, None], 0), axis=1).astype(BF16)
-    return fused_shards(act, *weights, counts)
+    return routed_shards(act, *weights, expert_ids, combine_ints)
 
 
 def solution(mesh):

time: 141 us -> 124 us (0.88)
  Pallas kernels: 132 us -> 122 us
  other arithmetic: 3.82 us -> 0 us
  local copies, waits for them, and re-layouts: 4.42 us -> 1.77 us
    pallas_call x1, Pallas kernels: 132 us -> 122 us  [fused_shards(): pl.pallas_call(functools.partial(fused_kernel, n, paired), out_shape=jax....]
    convert_element_type x2 -> x0, other arithmetic: 3.55 us -> none  [the longest x1 2.93 us: shards(): act = jax.nn.gelu(merger_input.astype(F32), approximate=False).astype(BF16)]
    reshape x2 -> x0, local copies, waits for them, and re-layouts: 1.78 us -> none  [fused_shards(): by_chip = act.reshape(rows, chips, 2 * depth).transpose(1, 0, 2)]
where the time goes in v2:
time: 124 us
  Pallas kernels  122 us (98%)
  local copies, waits for them, and re-layouts  1.77 us (1%)
    pallas_call x1, Pallas kernels, fused_shards(): pl.pallas_call(functools.partial(fused_kernel, n, paired), out_shape=jax....  122 us

profile of v2, /device:TPU:0, one launch (start us, length us, event | category | flops | bytes accessed | tf_op | source)
XLA Modules:
  0.0 123.6 jit_solution(8002341753384599933)
XLA Ops:
  0.0 121.8 %shard_map.91 = bf16[96,2048]{1,0:T(8,128)(2,1)} custom-call(bf16[96,2304]{1,0:T(8,128)(2,1)} %input_ref.1, s32[8,96]{1,0:T(8,128)} %bitcast.6, s32[8,96]{1,0:T(8,128)} %bitcast.7, f32[1,2048]{1,0:T(1,128)} %bitcast.4, f32[1,2048]{1,0:T(1,128)} %bitcast.5, bf16[144,2048]{1,0:T(8,128)(2,1)} %weight_hbm.1, bf16[1,2048,768]{2,1,0:T(8,128)(2,1)} %gate_hbm.1, ...), custom_call_target="tpu_custom_call" | custom-call | tf_op jit(solution)/shard_map/pallas_call | solution.py:421
  121.8 1.8 %copy.11 = bf16[96,2048]{1,0:T(8,128)(2,1)} copy(bf16[96,2048]{1,0:T(8,128)(2,1)} %shard_map.91) | data formatting | bytes 786432
